TPU v7x, 32 devices: a whole 2x2x4 slice. The times are simulated.
32 devices in a mesh: param: 8 (over y, x, core), proj: 4 (over z).
Axes of the slice: x: 2, y: 2, z: 4, core: 2. Of those that a mesh axis runs over, the one named last changes fastest.
Arguments:
- query_grads: float32 [256, 65536], P(None, 'param'), may hold values from -45 to 45, as said below
- stored: float32 [8192, 4096], P('param', 'proj'), may hold values from -6 to 6
- proj_seed: int32 [2], replicated, may hold values from 0 to 32748
- offsets: int32 [8], P('param'), may hold values from 0 to 32748
Outputs:
- similarity: float32 [256, 8192], P('proj', 'param')
Inputs may be any that keep to these rules, and one draw needn't show every extreme that they name: `query_grads`: query gradients have row and coordinate scales that differ.
All inputs are finite; a program needn't handle non-finite values.
Results may differ from a plain program's by a relative error of at most 0.0003.
Values sent between devices are 32-bit elements; how exact they have to be, the bound alone decides.
A program may use at most 128 MiB of HBM per device.

v0:
```python
import functools
import math

import jax
import jax.numpy as jnp
import numpy as np
from jax import lax
from jax.experimental import pallas as pl
from jax.experimental.pallas import tpu as pltpu
from jax.sharding import PartitionSpec as P

modulus = 32749
middle = modulus // 2
epsilon = 1e-06
bits = 8
block = 1 << bits
pairs = [(p, q) for p in range(bits) for q in range(p + 1, bits)]
slab_blocks = 4
slab = block * slab_blocks
chunk = 256
MESH = pl.DeviceIdType.MESH


def bit_features():
    digits = (np.arange(block)[:, None] >> np.arange(bits)[None, :]) & 1
    cross = np.stack([digits[:, p] * digits[:, q] for p, q in pairs], axis=1)
    vary = np.concatenate([digits, np.ones((block, 1), digits.dtype)], axis=1)
    out = np.zeros((block, 128), np.float32)
    for at in (0, 32):
        out[:, at : at + len(pairs)] = cross
    for at in (64, 80):
        out[:, at : at + bits + 1] = vary
    return jnp.asarray(out, jnp.bfloat16)


def pair_weights():
    out = np.zeros((32, 128), np.int32)
    for row, (p, q) in enumerate(pairs):
        out[row] = 2 ** (p + q + 1)
    return jnp.asarray(out)


def reduced(value):
    times = jnp.round(value.astype(jnp.float32) * (1.0 / modulus)).astype(jnp.int32)
    return value - times * modulus


def reduced_float(value):
    return value - jnp.round(value * (1.0 / modulus)) * modulus


def two_pieces(value):
    high = jnp.round(value * (1.0 / 128)) * 128.0
    return high.astype(jnp.bfloat16), (value - high).astype(jnp.bfloat16)


def split(value):
    high = value.astype(jnp.bfloat16)
    return high, (value - high.astype(jnp.float32)).astype(jnp.bfloat16)


def mix(a, b):
    return jnp.dot(a, b, preferred_element_type=jnp.float32)


def mix_rows(a, b):
    return lax.dot_general(a, b, (((1,), (1,)), ((), ())), preferred_element_type=jnp.float32)


def kernel(n_param, n_proj, offset_ref, seed_ref, feat_ref, weight_ref, grads_ref, stored_ref, out_ref,
           stage, store, high_q, low_q, cross, vary, high_a, low_a, high_b, low_b, total,
           part, pair_in, ring_in, proj, raw, square_out, square_in, column_sum, line_in, state, score_high, score_low,
           grad_sem, store_sem, pair_sem, ring_sem, gather_sem, back_sem, square_sem, line_sem):
    queries, coords = high_q.shape
    store_rows, width = store.shape
    slabs = coords // slab
    chunks = width // chunk
    chips = n_param // 2
    half = queries // 2
    own = half // chips
    share = queries // n_proj
    tile = min(store_rows, 256)
    tiles = store_rows // tile
    me = lax.axis_index("param")
    here = lax.axis_index("proj")
    core = lax.rem(me, 2)
    chip = lax.div(me, 2)
    sibling = me + 1 - 2 * core
    width_total = width * n_proj
    scale = 2.0 * math.sqrt(3.0 / (coords * n_param))

    def partner(o):
        return lax.rem(chip + o, chips)

    def fetch(s):
        return pltpu.make_async_copy(
            grads_ref.at[:, pl.ds(pl.multiple_of(s * slab, slab), slab)], stage.at[s], grad_sem.at[s]
        )

    for s in range(slabs):
        fetch(s).start()
    fetch_store = pltpu.make_async_copy(stored_ref, store, store_sem)
    fetch_store.start()

    barrier = pltpu.get_barrier_semaphore()
    pl.semaphore_signal(barrier, inc=1, device_id={"param": sibling}, device_id_type=MESH)
    for o in range(1, chips):
        pl.semaphore_signal(
            barrier, inc=1, device_id={"param": partner(o) * 2 + core}, device_id_type=MESH
        )
    for o in range(1, n_proj):
        pl.semaphore_signal(
            barrier, inc=1, device_id={"proj": lax.rem(here + o, n_proj)}, device_id_type=MESH
        )

    shape = (16, width)
    column = here * width + lax.broadcasted_iota(jnp.int32, shape, 1)
    row = lax.broadcasted_iota(jnp.int32, shape, 0)
    start = reduced(jnp.full(shape, offset_ref[0] * 1103 + seed_ref[0], jnp.int32))
    factor = reduced(column * 2111 + seed_ref[1]) + 1
    slope = reduced(factor * 1103)
    level = reduced((start + 3) * factor + 14)
    square = reduced(slope * slope)
    linear = reduced(reduced(slope * level) * 2 + 1103)
    constant = reduced(level * level + start)
    weights = jnp.concatenate([weight_ref[...]] * (width // 128), axis=1)
    pair_coef = reduced(jnp.concatenate([square, square], axis=0) * weights)
    high, low = two_pieces(pair_coef.astype(jnp.float32))
    cross[pl.ds(0, 32), :] = high
    cross[pl.ds(32, 32), :] = low
    power = jnp.where(row < bits, jnp.left_shift(1, jnp.minimum(row, bits)), 0)
    first = reduced(reduced(square * power) * power + linear * power)
    first = jnp.where(row == bits, reduced(constant - middle), first)
    twice = reduced(square * (2 * block))
    step = reduced(twice * power)
    leap = reduced(reduced(square * block) * block + linear * block)
    step = jnp.where(row == bits, leap, step)
    bend = jnp.where(row == bits, reduced(twice * block), 0)
    state[0] = first.astype(jnp.float32)
    state[1] = step.astype(jnp.float32)
    state[2] = bend.astype(jnp.float32)

    @pl.loop(0, coords // block)
    def _(i):
        value = state[0]
        step = state[1]
        high, low = two_pieces(value)
        vary[i, pl.ds(0, 16), :] = high
        vary[i, pl.ds(16, 16), :] = low
        state[0] = reduced_float(value + step)
        state[1] = reduced_float(step + state[2])

    def prepare(s):
        fetch(s).wait()
        at = pl.ds(pl.multiple_of(s * slab, slab), slab)
        high, low = split(stage[s])
        high_q[:, at] = high
        low_q[:, at] = low

    def make(t, high, low):
        s = lax.rem(t, slabs)
        at = pl.ds(pl.multiple_of(lax.div(t, slabs) * chunk, chunk), chunk)
        blank = jnp.zeros((32, chunk), jnp.bfloat16)
        for b in range(slab_blocks):
            coef = jnp.concatenate([cross[:, at], vary[s * slab_blocks + b, :, at], blank], axis=0)
            x = mix(feat_ref[...], coef) * (1.0 / modulus)
            top, rest = split(x - jnp.round(x))
            high[pl.ds(b * block, block), :] = top
            low[pl.ds(b * block, block), :] = rest

    def use(t, high, low):
        s = lax.rem(t, slabs)
        at = pl.ds(pl.multiple_of(s * slab, slab), slab)
        qh = high_q[:, at]
        wh = high[...]
        total[...] += mix(qh, wh) + mix(low_q[:, at], wh) + mix(qh, low[...])

    def cols(n):
        return pl.ds(pl.multiple_of(n * chunk, chunk), chunk)

    def pair_copy(n):
        return pltpu.make_async_remote_copy(
            src_ref=part.at[pl.ds(pl.multiple_of((1 - core) * half, half), half), cols(n)],
            dst_ref=pair_in.at[n], send_sem=pair_sem.at[0, n], recv_sem=pair_sem.at[1, n],
            device_id={"param": sibling}, device_id_type=MESH,
        )

    def ring_copy(n, o):
        to = partner(o)
        return pltpu.make_async_remote_copy(
            src_ref=part.at[pl.ds(pl.multiple_of(core * half + to * own, own), own), cols(n)],
            dst_ref=ring_in.at[n, o - 1],
            send_sem=ring_sem.at[0, n, o - 1], recv_sem=ring_sem.at[1, n, o - 1],
            device_id={"param": to * 2 + core}, device_id_type=MESH,
        )

    own_rows = pl.ds(pl.multiple_of(core * half + chip * own, own), own)
    half_rows = pl.ds(pl.multiple_of(core * half, half), half)

    def gather_copy(n, o):
        return pltpu.make_async_remote_copy(
            src_ref=proj.at[own_rows, cols(n)], dst_ref=proj.at[own_rows, cols(n)],
            send_sem=gather_sem.at[0, n, o - 1], recv_sem=gather_sem.at[1, n, o - 1],
            device_id={"param": partner(o) * 2 + core}, device_id_type=MESH,
        )

    def back_copy(n):
        return pltpu.make_async_remote_copy(
            src_ref=proj.at[half_rows, cols(n)], dst_ref=proj.at[half_rows, cols(n)],
            send_sem=back_sem.at[0, n], recv_sem=back_sem.at[1, n],
            device_id={"param": sibling}, device_id_type=MESH,
        )

    def begin(n):
        column = here * width + n * chunk + lax.broadcasted_iota(jnp.int32, (1, chunk), 1)
        gain = jnp.sqrt(1.0 + column.astype(jnp.float32) * (2.0 / width_total)) * scale
        part[:, cols(n)] = total[...] * gain
        total[...] = jnp.zeros_like(total)
        pair_copy(n).start()

    def spread(n):
        pair_copy(n).wait_recv()
        part[half_rows, cols(n)] += pair_in[n]
        for o in range(1, chips):
            ring_copy(n, o).start()

    def join(n):
        value = part[own_rows, cols(n)]
        for o in range(1, chips):
            ring_copy(n, o).wait_recv()
            value += ring_in[n, o - 1]
        proj[own_rows, cols(n)] = value
        for o in range(1, chips):
            gather_copy(n, o).start()

    def hand_back(n):
        for o in range(1, chips):
            gather_copy(n, o).wait_recv()
        back_copy(n).start()

    def sums(n):
        back_copy(n).wait_recv()
        value = proj[:, cols(n)]
        high, low = split(value)
        score_high[...] = high
        score_low[...] = low
        squares = jnp.sum(value * value, axis=1, keepdims=True)
        column_sum[...] += jnp.broadcast_to(squares, (queries, 128))

    def score(n, r):
        at = pl.ds(pl.multiple_of(r * tile, tile), tile)
        sh, sl = split(store[at, cols(n)])
        high = score_high[...]
        raw[:, at] += mix_rows(high, sh) + mix_rows(score_low[...], sh) + mix_rows(high, sl)

    def scores(n):
        sums(n)

        @pl.loop(0, tiles)
        def _(r):
            score(n, r)

    def square_copy(o):
        return pltpu.make_async_remote_copy(
            src_ref=square_out, dst_ref=square_in.at[o - 1],
            send_sem=square_sem.at[0, o - 1], recv_sem=square_sem.at[1, o - 1],
            device_id={"proj": lax.rem(here + o, n_proj)}, device_id_type=MESH,
        )

    def piece(goal, p):
        return (
            pl.ds(pl.multiple_of(goal * share, share), share),
            pl.ds(pl.multiple_of(p * tile, tile), tile),
        )

    def line_copy(way, goal, p):
        return pltpu.make_async_remote_copy(
            src_ref=raw.at[piece(goal, p)], dst_ref=line_in.at[way, goal, p],
            send_sem=line_sem.at[0, way, goal, p], recv_sem=line_sem.at[1, way, goal, p],
            device_id={"proj": lax.rem(here + 1 - 2 * way + n_proj, n_proj)}, device_id_type=MESH,
        )

    def arrived(way, goal, p):
        line_copy(way, goal, p).wait_recv()
        raw[piece(goal, p)] += line_in[way, goal, p]

    late = (here >= (n_proj + 1) // 2).astype(jnp.int32)

    def moves(k, way):
        goal = (1 - way) * (n_proj - 1 - k) + way * k
        ahead = (goal - here) * (1 - 2 * way)
        behind = (1 - way) * here + way * (n_proj - 1 - here)
        return goal, ahead, behind

    total[...] = jnp.zeros_like(total)
    raw[...] = jnp.zeros_like(raw)
    column_sum[...] = jnp.zeros_like(column_sum)
    make(0, high_a, low_a)
    pl.semaphore_wait(barrier, n_param // 2 + n_proj - 1)
    turns = slabs // 2

    @pl.loop(0, chunks * turns)
    def _(it):
        t = it * 2

        @pl.when(it < turns)
        def _():
            prepare(t)
            prepare(t + 1)

        make(t + 1, high_b, low_b)
        use(t, high_a, low_a)
        make(jnp.minimum(t + 2, chunks * slabs - 1), high_a, low_a)
        use(t + 1, high_b, low_b)

        def after(delay, stage_of):
            turn = it - delay - (turns - 1)

            @pl.when((turn >= 0) & (lax.rem(turn + turns, turns) == 0))
            def _():
                stage_of(lax.div(turn, turns))

        after(0, begin)
        after(1, spread)
        after(3, join)
        after(5, hand_back)

        @pl.when(it == turns + 1)
        def _():
            fetch_store.wait()

        after(7, scores)

    last = chunks - 1
    spread(last)
    hand_back(last - 1)
    scores(last - 1)
    join(last)
    hand_back(last)
    sums(last)

    square_out[...] = column_sum[...].T[:8, :]
    for o in range(1, n_proj):
        square_copy(o).start()

    @pl.loop(0, tiles)
    def _(p):
        score(last, p)

        @pl.loop(0, n_proj - 1)
        def _(k):
            for way in range(2):
                goal, ahead, behind = moves(k, way)

                @pl.when((behind == 0) & (ahead > 0))
                def _():
                    line_copy(way, goal, p).start()

    def forward(way, p):
        @pl.loop(0, n_proj - 1)
        def _(k):
            goal, ahead, behind = moves(k, way)

            @pl.when((ahead > 0) & (behind > 0))
            def _():
                arrived(way, goal, p)
                line_copy(way, goal, p).start()

    @pl.loop(0, tiles + 1)
    def _(p):
        @pl.when(p < tiles)
        def _():
            forward(late, p)

        @pl.when(p > 0)
        def _():
            forward(1 - late, p - 1)

    whole = column_sum[...].T[:8, :]
    for o in range(1, n_proj):
        square_copy(o).wait_recv()
        whole += square_in[o - 1]
    inverse = lax.rsqrt(whole * (1.0 / width_total) + epsilon) * (1.0 / math.sqrt(width_total))
    column_sum[...] = jnp.broadcast_to(inverse[:1, :], (128, queries)).T

    @pl.loop(0, tiles)
    def _(p):
        @pl.when(here > 0)
        def _():
            arrived(0, here, p)

        @pl.when(here < n_proj - 1)
        def _():
            arrived(1, here, p)

        rows, at = piece(here, p)
        out_ref[:, at] = jnp.tanh(raw[rows, at] * column_sum[rows, :][:, :1])

    @pl.loop(0, chunks)
    def _(n):
        pair_copy(n).wait_send()
        back_copy(n).wait_send()
        for o in range(1, chips):
            ring_copy(n, o).wait_send()
            gather_copy(n, o).wait_send()

    for o in range(1, n_proj):
        square_copy(o).wait_send()

    @pl.loop(0, tiles)
    def _(p):
        @pl.loop(0, n_proj - 1)
        def _(k):
            for way in range(2):
                goal, ahead, behind = moves(k, way)

                @pl.when(ahead > 0)
                def _():
                    line_copy(way, goal, p).wait_send()


def on_device(query_grads, stored, proj_seed, offsets):
    n_param = lax.axis_size("param")
    n_proj = lax.axis_size("proj")
    queries, coords = query_grads.shape
    store_rows, width = stored.shape
    chips = n_param // 2
    chunks = width // chunk
    slabs = coords // slab
    share = queries // n_proj
    own = queries // n_param
    tile = min(store_rows, 256)
    tiles = store_rows // tile
    vmem = pl.BlockSpec(memory_space=pltpu.VMEM)
    smem = pl.BlockSpec(memory_space=pltpu.SMEM)
    hbm = pl.BlockSpec(memory_space=pl.ANY)
    weight = pltpu.VMEM((slab, chunk), jnp.bfloat16)
    dma = pltpu.SemaphoreType.DMA
    return pl.pallas_call(
        functools.partial(kernel, n_param, n_proj),
        out_shape=jax.ShapeDtypeStruct((share, store_rows), jnp.float32),
        in_specs=[smem, smem, vmem, vmem, hbm, hbm],
        out_specs=vmem,
        scratch_shapes=[
            pltpu.VMEM((slabs, queries, slab), jnp.float32),
            pltpu.VMEM((store_rows, width), jnp.float32),
            pltpu.VMEM((queries, coords), jnp.bfloat16),
            pltpu.VMEM((queries, coords), jnp.bfloat16),
            pltpu.VMEM((64, width), jnp.bfloat16),
            pltpu.VMEM((coords // block, 32, width), jnp.bfloat16),
            weight, weight, weight, weight,
            pltpu.VMEM((queries, chunk), jnp.float32),
            pltpu.VMEM((queries, width), jnp.float32),
            pltpu.VMEM((chunks, queries // 2, chunk), jnp.float32),
            pltpu.VMEM((chunks, chips - 1, own, chunk), jnp.float32),
            pltpu.VMEM((queries, width), jnp.float32),
            pltpu.VMEM((queries, store_rows), jnp.float32),
            pltpu.VMEM((8, queries), jnp.float32),
            pltpu.VMEM((n_proj - 1, 8, queries), jnp.float32),
            pltpu.VMEM((queries, 128), jnp.float32),
            pltpu.VMEM((2, n_proj, tiles, share, tile), jnp.float32),
            pltpu.VMEM((3, 16, width), jnp.float32),
            pltpu.VMEM((queries, chunk), jnp.bfloat16),
            pltpu.VMEM((queries, chunk), jnp.bfloat16),
            dma((slabs,)),
            dma,
            dma((2, chunks)),
            dma((2, chunks, chips - 1)),
            dma((2, chunks, chips - 1)),
            dma((2, chunks)),
            dma((2, n_proj - 1)),
            dma((2, 2, n_proj, tiles)),
        ],
        compiler_params=pltpu.CompilerParams(
            collective_id=0, has_side_effects=True, vmem_limit_bytes=58 * 1024 * 1024
        ),
        name="attribution",
    )(offsets, proj_seed, bit_features(), pair_weights(), query_grads, stored)


def solution(mesh):
    placed = (P(None, "param"), P("param", "proj"), P(), P("param"))
    return jax.shard_map(
        on_device, mesh=mesh, in_specs=placed, out_specs=P("proj", "param"), check_vma=False
    )
```

profile of v0, /device:TPU:0, one launch (start us, length us, event | category | flops | bytes accessed | tf_op | source)
XLA Modules:
  0.0 71.4 jit_solution(3526941030628438026)
XLA Ops:
  0.7 69.0 %attribution.1 = f32[64,1024]{1,0:T(8,128)} custom-call(s32[1]{0:T(128)S(6)} %copy.8.offset_ref, s32[2]{0:T(128)} %seed_ref.1, bf16[256,128]{1,0:T(8,128)(2,1)} %constant.4.clone.feat_ref, s32[32,128]{1,0:T(8,128)} %constant.5.clone.weight_ref, f32[256,8192]{1,0:T(8,128)} %grads_ref.1, f32[1024,1024]{1,0:T(8,128)} %stored_ref.1), custom_call_target="tpu_custom_call" | custom-call | tf_op jit(solution)/shard_map/attribution/pallas_call | solution.py:439
  69.7 1.7 %copy.9 = f32[64,1024]{1,0:T(8,128)} copy(f32[64,1024]{1,0:T(8,128)} %attribution.1) | data formatting | bytes 524288
where the time goes:
time: 71.6 us; the launch traced here: 71.4 us
  Pallas kernels  69 us (96%)
  local copies, waits for them, and re-layouts  1.67 us (2%)
    pallas_call x1, Pallas kernels, on_device(): pl.pallas_call(functools.partial(kernel, n_param, n_proj), out_shape=jax....  69 us
    unnamed x1, local copies, waits for them, and re-layouts  1.67 us

commit v1 on v0

--- a/solution.py
+++ b/solution.py
@@ -12,10 +12,11 @@
 modulus = 32749
 middle = modulus // 2
 epsilon = 1e-06
-bits = 8
+bits = 9
 block = 1 << bits
 pairs = [(p, q) for p in range(bits) for q in range(p + 1, bits)]
-slab_blocks = 4
+slab_blocks = 2
+cross_rows = 48
 slab = block * slab_blocks
 chunk = 256
 MESH = pl.DeviceIdType.MESH
@@ -26,15 +27,15 @@
     cross = np.stack([digits[:, p] * digits[:, q] for p, q in pairs], axis=1)
     vary = np.concatenate([digits, np.ones((block, 1), digits.dtype)], axis=1)
     out = np.zeros((block, 128), np.float32)
-    for at in (0, 32):
+    for at in (0, cross_rows):
         out[:, at : at + len(pairs)] = cross
-    for at in (64, 80):
+    for at in (2 * cross_rows, 2 * cross_rows + 16):
         out[:, at : at + bits + 1] = vary
     return jnp.asarray(out, jnp.bfloat16)
 
 
 def pair_weights():
-    out = np.zeros((32, 128), np.int32)
+    out = np.zeros((cross_rows, 128), np.int32)
     for row, (p, q) in enumerate(pairs):
         out[row] = 2 ** (p + q + 1)
     return jnp.asarray(out)
@@ -68,10 +69,10 @@
 
 
 def kernel(n_param, n_proj, offset_ref, seed_ref, feat_ref, weight_ref, grads_ref, stored_ref, out_ref,
-           stage, store, high_q, low_q, cross, vary, high_a, low_a, high_b, low_b, total,
+           stage, store, both_q, cross, vary, high_a, low_a, high_b, low_b, total,
            part, pair_in, ring_in, proj, raw, square_out, square_in, column_sum, line_in, state, score_high, score_low,
            grad_sem, store_sem, pair_sem, ring_sem, gather_sem, back_sem, square_sem, line_sem):
-    queries, coords = high_q.shape
+    queries, coords = both_q.shape[0] // 2, both_q.shape[1]
     store_rows, width = store.shape
     slabs = coords // slab
     chunks = width // chunk
@@ -124,10 +125,10 @@
     linear = reduced(reduced(slope * level) * 2 + 1103)
     constant = reduced(level * level + start)
     weights = jnp.concatenate([weight_ref[...]] * (width // 128), axis=1)
-    pair_coef = reduced(jnp.concatenate([square, square], axis=0) * weights)
+    pair_coef = reduced(jnp.concatenate([square] * (cross_rows // 16), axis=0) * weights)
     high, low = two_pieces(pair_coef.astype(jnp.float32))
-    cross[pl.ds(0, 32), :] = high
-    cross[pl.ds(32, 32), :] = low
+    cross[pl.ds(0, cross_rows), :] = high
+    cross[pl.ds(cross_rows, cross_rows), :] = low
     power = jnp.where(row < bits, jnp.left_shift(1, jnp.minimum(row, bits)), 0)
     first = reduced(reduced(square * power) * power + linear * power)
     first = jnp.where(row == bits, reduced(constant - middle), first)
@@ -154,15 +155,14 @@
         fetch(s).wait()
         at = pl.ds(pl.multiple_of(s * slab, slab), slab)
         high, low = split(stage[s])
-        high_q[:, at] = high
-        low_q[:, at] = low
+        both_q[pl.ds(0, queries), at] = high
+        both_q[pl.ds(queries, queries), at] = low
 
     def make(t, high, low):
         s = lax.rem(t, slabs)
         at = pl.ds(pl.multiple_of(lax.div(t, slabs) * chunk, chunk), chunk)
-        blank = jnp.zeros((32, chunk), jnp.bfloat16)
         for b in range(slab_blocks):
-            coef = jnp.concatenate([cross[:, at], vary[s * slab_blocks + b, :, at], blank], axis=0)
+            coef = jnp.concatenate([cross[:, at], vary[s * slab_blocks + b, :, at]], axis=0)
             x = mix(feat_ref[...], coef) * (1.0 / modulus)
             top, rest = split(x - jnp.round(x))
             high[pl.ds(b * block, block), :] = top
@@ -171,9 +171,9 @@
     def use(t, high, low):
         s = lax.rem(t, slabs)
         at = pl.ds(pl.multiple_of(s * slab, slab), slab)
-        qh = high_q[:, at]
-        wh = high[...]
-        total[...] += mix(qh, wh) + mix(low_q[:, at], wh) + mix(qh, low[...])
+        main = mix(both_q[:, at], high[...])
+        rest = mix(both_q[pl.ds(0, queries), at], low[...])
+        total[...] += main[:queries] + (main[queries:] + rest)
 
     def cols(n):
         return pl.ds(pl.multiple_of(n * chunk, chunk), chunk)
@@ -444,9 +444,8 @@
         scratch_shapes=[
             pltpu.VMEM((slabs, queries, slab), jnp.float32),
             pltpu.VMEM((store_rows, width), jnp.float32),
-            pltpu.VMEM((queries, coords), jnp.bfloat16),
-            pltpu.VMEM((queries, coords), jnp.bfloat16),
-            pltpu.VMEM((64, width), jnp.bfloat16),
+            pltpu.VMEM((2 * queries, coords), jnp.bfloat16),
+            pltpu.VMEM((2 * cross_rows, width), jnp.bfloat16),
             pltpu.VMEM((coords // block, 32, width), jnp.bfloat16),
             weight, weight, weight, weight,
             pltpu.VMEM((queries, chunk), jnp.float32),

time: 71.6 us -> 71.5 us (level)
  no operation moved by 1% of the time
where the time goes in v1:
time: 71.5 us; the launch traced here: 71.3 us
  Pallas kernels  69 us (97%)
  local copies, waits for them, and re-layouts  1.67 us (2%)
    pallas_call x1, Pallas kernels, on_device(): pl.pallas_call(functools.partial(kernel, n_param, n_proj), out_shape=jax....  69 us
    unnamed x1, local copies, waits for them, and re-layouts  1.67 us

profile of v1, /device:TPU:0, one launch (start us, length us, event | category | flops | bytes accessed | tf_op | source)
XLA Modules:
  0.0 71.3 jit_solution(5209568444163382352)
XLA Ops:
  0.7 69.0 %attribution.1 = f32[64,1024]{1,0:T(8,128)} custom-call(s32[1]{0:T(128)S(6)} %copy.8.offset_ref, s32[2]{0:T(128)} %seed_ref.1, bf16[512,128]{1,0:T(8,128)(2,1)} %constant.4.clone.feat_ref, s32[48,128]{1,0:T(8,128)} %constant.5.clone.weight_ref, f32[256,8192]{1,0:T(8,128)} %grads_ref.1, f32[1024,1024]{1,0:T(8,128)} %stored_ref.1), custom_call_target="tpu_custom_call" | custom-call | tf_op jit(solution)/shard_map/attribution/pallas_call | solution.py:439
  69.6 1.7 %copy.9 = f32[64,1024]{1,0:T(8,128)} copy(f32[64,1024]{1,0:T(8,128)} %attribution.1) | data formatting | bytes 524288

commit v2 on v1

--- a/solution.py
+++ b/solution.py
@@ -17,6 +17,7 @@
 pairs = [(p, q) for p in range(bits) for q in range(p + 1, bits)]
 slab_blocks = 2
 cross_rows = 48
+to_whole = 1.5 * 2**23
 slab = block * slab_blocks
 chunk = 256
 MESH = pl.DeviceIdType.MESH
@@ -47,11 +48,11 @@
 
 
 def reduced_float(value):
-    return value - jnp.round(value * (1.0 / modulus)) * modulus
+    return value - ((value * (1.0 / modulus) + to_whole) - to_whole) * modulus
 
 
 def two_pieces(value):
-    high = jnp.round(value * (1.0 / 128)) * 128.0
+    high = ((value * (1.0 / 128) + to_whole) - to_whole) * 128.0
     return high.astype(jnp.bfloat16), (value - high).astype(jnp.bfloat16)
 
 
@@ -164,7 +165,7 @@
         for b in range(slab_blocks):
             coef = jnp.concatenate([cross[:, at], vary[s * slab_blocks + b, :, at]], axis=0)
             x = mix(feat_ref[...], coef) * (1.0 / modulus)
-            top, rest = split(x - jnp.round(x))
+            top, rest = split(x - ((x + to_whole) - to_whole))
             high[pl.ds(b * block, block), :] = top
             low[pl.ds(b * block, block), :] = rest
 

time: 71.5 us -> 72.3 us (1.011)
  Pallas kernels: 69 us -> 69.8 us
    pallas_call x1, Pallas kernels: 69 us -> 69.8 us  [on_device(): pl.pallas_call(functools.partial(kernel, n_param, n_proj), out_shape=jax....]
where the time goes in v2:
time: 72.3 us; the launch traced here: 72.1 us
  Pallas kernels  69.8 us (97%)
  local copies, waits for them, and re-layouts  1.67 us (2%)
    pallas_call x1, Pallas kernels, on_device(): pl.pallas_call(functools.partial(kernel, n_param, n_proj), out_shape=jax....  69.8 us
    unnamed x1, local copies, waits for them, and re-layouts  1.67 us

profile of v2, /device:TPU:0, one launch (start us, length us, event | category | flops | bytes accessed | tf_op | source)
XLA Modules:
  0.0 72.1 jit_solution(16190519058886283368)
XLA Ops:
  0.7 69.8 %attribution.1 = f32[64,1024]{1,0:T(8,128)} custom-call(s32[1]{0:T(128)S(6)} %copy.8.offset_ref, s32[2]{0:T(128)} %seed_ref.1, bf16[512,128]{1,0:T(8,128)(2,1)} %constant.4.clone.feat_ref, s32[48,128]{1,0:T(8,128)} %constant.5.clone.weight_ref, f32[256,8192]{1,0:T(8,128)} %grads_ref.1, f32[1024,1024]{1,0:T(8,128)} %stored_ref.1), custom_call_target="tpu_custom_call" | custom-call | tf_op jit(solution)/shard_map/attribution/pallas_call | solution.py:440
  70.4 1.7 %copy.9 = f32[64,1024]{1,0:T(8,128)} copy(f32[64,1024]{1,0:T(8,128)} %attribution.1) | data formatting | bytes 524288

commit v3 on v1

--- a/solution.py
+++ b/solution.py
@@ -82,6 +82,8 @@
     share = queries // n_proj
     tile = min(store_rows, 256)
     tiles = store_rows // tile
+    strip = min(store_rows, 128)
+    strips = store_rows // strip
     me = lax.axis_index("param")
     here = lax.axis_index("proj")
     core = lax.rem(me, 2)
@@ -270,7 +272,7 @@
     def piece(goal, p):
         return (
             pl.ds(pl.multiple_of(goal * share, share), share),
-            pl.ds(pl.multiple_of(p * tile, tile), tile),
+            pl.ds(pl.multiple_of(p * strip, strip), strip),
         )
 
     def line_copy(way, goal, p):
@@ -346,15 +348,16 @@
     @pl.loop(0, tiles)
     def _(p):
         score(last, p)
-
-        @pl.loop(0, n_proj - 1)
-        def _(k):
-            for way in range(2):
-                goal, ahead, behind = moves(k, way)
-
-                @pl.when((behind == 0) & (ahead > 0))
-                def _():
-                    line_copy(way, goal, p).start()
+        for sub in range(strips // tiles):
+
+            @pl.loop(0, n_proj - 1)
+            def _(k):
+                for way in range(2):
+                    goal, ahead, behind = moves(k, way)
+
+                    @pl.when((behind == 0) & (ahead > 0))
+                    def _():
+                        line_copy(way, goal, p * (strips // tiles) + sub).start()
 
     def forward(way, p):
         @pl.loop(0, n_proj - 1)
@@ -366,9 +369,9 @@
                 arrived(way, goal, p)
                 line_copy(way, goal, p).start()
 
-    @pl.loop(0, tiles + 1)
+    @pl.loop(0, strips + 1)
     def _(p):
-        @pl.when(p < tiles)
+        @pl.when(p < strips)
         def _():
             forward(late, p)
 
@@ -383,7 +386,7 @@
     inverse = lax.rsqrt(whole * (1.0 / width_total) + epsilon) * (1.0 / math.sqrt(width_total))
     column_sum[...] = jnp.broadcast_to(inverse[:1, :], (128, queries)).T
 
-    @pl.loop(0, tiles)
+    @pl.loop(0, strips)
     def _(p):
         @pl.when(here > 0)
         def _():
@@ -407,7 +410,7 @@
     for o in range(1, n_proj):
         square_copy(o).wait_send()
 
-    @pl.loop(0, tiles)
+    @pl.loop(0, strips)
     def _(p):
         @pl.loop(0, n_proj - 1)
         def _(k):
@@ -431,6 +434,8 @@
     own = queries // n_param
     tile = min(store_rows, 256)
     tiles = store_rows // tile
+    strip = min(store_rows, 128)
+    strips = store_rows // strip
     vmem = pl.BlockSpec(memory_space=pltpu.VMEM)
     smem = pl.BlockSpec(memory_space=pltpu.SMEM)
     hbm = pl.BlockSpec(memory_space=pl.ANY)
@@ -457,7 +462,7 @@
             pltpu.VMEM((8, queries), jnp.float32),
             pltpu.VMEM((n_proj - 1, 8, queries), jnp.float32),
             pltpu.VMEM((queries, 128), jnp.float32),
-            pltpu.VMEM((2, n_proj, tiles, share, tile), jnp.float32),
+            pltpu.VMEM((2, n_proj, strips, share, strip), jnp.float32),
             pltpu.VMEM((3, 16, width), jnp.float32),
             pltpu.VMEM((queries, chunk), jnp.bfloat16),
             pltpu.VMEM((queries, chunk), jnp.bfloat16),
@@ -468,7 +473,7 @@
             dma((2, chunks, chips - 1)),
             dma((2, chunks)),
             dma((2, n_proj - 1)),
-            dma((2, 2, n_proj, tiles)),
+            dma((2, 2, n_proj, strips)),
         ],
         compiler_params=pltpu.CompilerParams(
             collective_id=0, has_side_effects=True, vmem_limit_bytes=58 * 1024 * 1024

time: 71.5 us -> 71.9 us (level)
  no operation moved by 1% of the time
where the time goes in v3:
time: 71.9 us; the launch traced here: 71.7 us
  Pallas kernels  69.4 us (97%)
  local copies, waits for them, and re-layouts  1.67 us (2%)
    pallas_call x1, Pallas kernels, on_device(): pl.pallas_call(functools.partial(kernel, n_param, n_proj), out_shape=jax....  69.4 us
    unnamed x1, local copies, waits for them, and re-layouts  1.67 us

profile of v3, /device:TPU:0, one launch (start us, length us, event | category | flops | bytes accessed | tf_op | source)
XLA Modules:
  0.0 71.7 jit_solution(17002787344699787705)
XLA Ops:
  0.7 69.4 %attribution.1 = f32[64,1024]{1,0:T(8,128)} custom-call(s32[1]{0:T(128)S(6)} %copy.8.offset_ref, s32[2]{0:T(128)} %seed_ref.1, bf16[512,128]{1,0:T(8,128)(2,1)} %constant.4.clone.feat_ref, s32[48,128]{1,0:T(8,128)} %constant.5.clone.weight_ref, f32[256,8192]{1,0:T(8,128)} %grads_ref.1, f32[1024,1024]{1,0:T(8,128)} %stored_ref.1), custom_call_target="tpu_custom_call" | custom-call | tf_op jit(solution)/shard_map/attribution/pallas_call | solution.py:444
  70.1 1.7 %copy.9 = f32[64,1024]{1,0:T(8,128)} copy(f32[64,1024]{1,0:T(8,128)} %attribution.1) | data formatting | bytes 524288

commit v4 on v1

--- a/solution.py
+++ b/solution.py
@@ -244,6 +244,9 @@
         high, low = split(value)
         score_high[...] = high
         score_low[...] = low
+
+    def squares_of(n):
+        value = proj[:, cols(n)]
         squares = jnp.sum(value * value, axis=1, keepdims=True)
         column_sum[...] += jnp.broadcast_to(squares, (queries, 128))
 
@@ -255,6 +258,7 @@
 
     def scores(n):
         sums(n)
+        squares_of(n)
 
         @pl.loop(0, tiles)
         def _(r):
@@ -339,10 +343,6 @@
     hand_back(last)
     sums(last)
 
-    square_out[...] = column_sum[...].T[:8, :]
-    for o in range(1, n_proj):
-        square_copy(o).start()
-
     @pl.loop(0, tiles)
     def _(p):
         score(last, p)
@@ -355,6 +355,13 @@
                 @pl.when((behind == 0) & (ahead > 0))
                 def _():
                     line_copy(way, goal, p).start()
+
+        @pl.when(p == 0)
+        def _():
+            squares_of(last)
+            square_out[...] = column_sum[...].T[:8, :]
+            for o in range(1, n_proj):
+                square_copy(o).start()
 
     def forward(way, p):
         @pl.loop(0, n_proj - 1)

time: 71.5 us -> 71.8 us (level)
  no operation moved by 1% of the time
where the time goes in v4:
time: 71.8 us; the launch traced here: 71.6 us
  Pallas kernels  69.3 us (97%)
  local copies, waits for them, and re-layouts  1.67 us (2%)
    pallas_call x1, Pallas kernels, on_device(): pl.pallas_call(functools.partial(kernel, n_param, n_proj), out_shape=jax....  69.3 us
    unnamed x1, local copies, waits for them, and re-layouts  1.67 us

profile of v4, /device:TPU:0, one launch (start us, length us, event | category | flops | bytes accessed | tf_op | source)
XLA Modules:
  0.0 71.6 jit_solution(10692566923511969833)
XLA Ops:
  0.7 69.3 %attribution.1 = f32[64,1024]{1,0:T(8,128)} custom-call(s32[1]{0:T(128)S(6)} %copy.8.offset_ref, s32[2]{0:T(128)} %seed_ref.1, bf16[512,128]{1,0:T(8,128)(2,1)} %constant.4.clone.feat_ref, s32[48,128]{1,0:T(8,128)} %constant.5.clone.weight_ref, f32[256,8192]{1,0:T(8,128)} %grads_ref.1, f32[1024,1024]{1,0:T(8,128)} %stored_ref.1), custom_call_target="tpu_custom_call" | custom-call | tf_op jit(solution)/shard_map/attribution/pallas_call | solution.py:446
  69.9 1.7 %copy.9 = f32[64,1024]{1,0:T(8,128)} copy(f32[64,1024]{1,0:T(8,128)} %attribution.1) | data formatting | bytes 524288
